TPU v7x, 32 devices: a whole 2x2x4 slice. The times are simulated.
32 devices in a mesh: group: 2 (over y), expert: 8 (over z, x), tensor: 2 (over core).
Axes of the slice: x: 2, y: 2, z: 4, core: 2. Of those that a mesh axis runs over, the one named last changes fastest.
Arguments:
- tokens: bfloat16 [64, 5120], P(('group', 'expert'), 'tensor'), parts along dimension 0, may hold values from -6 to 6
- expert_ids: int32 [64, 1], P(('group', 'expert')), parts along dimension 0, may hold values from 0 to 3; in each aligned block of 4 rows (0 to 3, 4 to 7, ...) at most 2 rows name the same one
- route_scale: float32 [64], P(('group', 'expert')), parts along dimension 0, may hold values from 0.1 to 1
- gate_weight: bfloat16 [8, 5120, 4096], P('expert', None, 'tensor'), may hold values from -0.078125 to 0.078125
- up_weight: bfloat16 [8, 5120, 4096], P('expert', None, 'tensor'), may hold values from -0.078125 to 0.078125
- down_weight: bfloat16 [8, 4096, 5120], P('expert', 'tensor'), may hold values from -0.0625 to 0.0625
Outputs:
- routed: bfloat16 [64, 5120], P(('group', 'expert'), 'tensor'), parts along dimension 0
There are 2 independent parts, one for each index of `group`. A program takes and returns all parts, laid end to end along the dimension named above; an argument that names none is the same for every part. Nothing has to cross between parts.
Inputs may be any that keep to these rules, and one draw needn't show every extreme that they name: `expert_ids`: ids of experts 0 to 3. In each aligned block of 4 rows (the rows of one index of the expert axis) no expert is named by more than 2 rows, a bound that some block reaches.
All inputs are finite; a program needn't handle non-finite values.
Results may differ from a plain program's by a relative error of at most 0.0051.
Values may be sent and summed in bfloat16 or wider, within the bound.
A program may use at most 192 MiB of HBM per device.

v0:
```python
import jax
import jax.numpy as jnp
from jax import lax
from jax.sharding import PartitionSpec as P

NE = 4
CAP = 2


def local(tokens, expert_ids, route_scale, gate_weight, up_weight, down_weight):
    devices_expert = lax.axis_size("expert")
    per_expert = devices_expert // NE
    tok_rows = tokens.shape[0]
    capacity = CAP
    width = gate_weight.shape[1]
    ids = expert_ids[:, 0]
    same_expert = ids[:, None] == ids[None, :]
    positions = jnp.arange(tok_rows, dtype=jnp.int32)
    earlier = positions[None, :] < positions[:, None]
    slot_index = jnp.sum((same_expert & earlier).astype(jnp.int32), axis=1)
    key_index = ids * capacity + slot_index
    table = (key_index[None, :] == jnp.arange(NE * capacity, dtype=jnp.int32)[:, None]).astype(
        jnp.bfloat16
    )
    w_gate = gate_weight[0]
    w_up = up_weight[0]
    w_down = down_weight[0]
    whole = lax.all_gather(tokens, "tensor", axis=1, tiled=True)
    placed = jnp.dot(table, whole, preferred_element_type=jnp.float32).astype(jnp.bfloat16)
    placed = placed.reshape(NE, capacity, whole.shape[1])
    received = lax.all_to_all(
        jnp.repeat(placed, per_expert, axis=0), "expert", split_axis=0, concat_axis=0, tiled=True
    )
    flat = received.reshape(-1, width)
    gate = jnp.dot(flat, w_gate, preferred_element_type=jnp.float32)
    up_part = jnp.dot(flat, w_up, preferred_element_type=jnp.float32)
    hidden = (jax.nn.silu(gate) * up_part).astype(jnp.bfloat16)
    partial_value = jnp.dot(hidden, w_down, preferred_element_type=jnp.float32)
    partial_value = partial_value.reshape(received.shape[0], received.shape[1], width)
    returned = lax.all_to_all(partial_value, "expert", split_axis=0, concat_axis=0, tiled=True)
    summed = (
        returned.reshape(NE, per_expert, capacity, width).sum(axis=1).reshape(NE * capacity, width)
    )
    mine = jnp.take(summed, key_index, axis=0)
    shares = lax.psum_scatter(mine, "tensor", scatter_dimension=1, tiled=True)
    return (shares * route_scale[:, None]).astype(jnp.bfloat16)


def solution(mesh):
    in_specs = (
        P(("group", "expert"), "tensor"),
        P(("group", "expert"), None),
        P(("group", "expert")),
        P("expert", None, "tensor"),
        P("expert", None, "tensor"),
        P("expert", "tensor", None),
    )
    out_specs = P(("group", "expert"), "tensor")
    return jax.shard_map(local, mesh=mesh, in_specs=in_specs, out_specs=out_specs, check_vma=False)
```

profile of v0, /device:TPU:0, one launch (start us, length us, event | category | flops | bytes accessed | tf_op | source)
XLA Modules:
  0.0 85.6 jit_solution(6080527115065380495)
XLA Ops:
  6.5 0.9 %convert_reduce_fusion = s32[4]{0:T(128)S(1)} fusion(s32[4]{0:T(128)} %bitcast.36), kind=kLoop, calls=%fused_computation.18 | loop fusion | flops 76 | bytes 32 | tf_op jit(solution)/shard_map/reduce_sum | solution.py:20
  7.4 0.7 multiply_add_fusion
  8.1 2.1 %all_gather.3 = bf16[4,5120]{1,0:T(4,128)(2,1)S(1)} all-gather(bf16[4,2560]{1,0:T(4,128)(2,1)} %param.6), channel_id=1, replica_groups=mesh['group'=2,'expert'=8,'tensor'=2] {'tensor'}, dimensions={1}, use_global_device_ids=true | all-gather | bytes 61440 | tf_op jit(solution)/shard_map/all_gather | solution.py:28
  10.3 0.1 convolution_convert_fusion
  10.4 0.1 broadcast_in_dim.19
  10.5 14.7 %all_to_all.10 = bf16[8,2,5120]{2,1,0:T(2,128)(2,1)S(1)} all-to-all(bf16[8,2,5120]{2,1,0:T(2,128)(2,1)S(1)} %bitcast.34), channel_id=1, replica_groups=mesh['group'=2,'expert'=8,'tensor'=2] {'expert'}, dimensions={0} | all-to-all | bytes 327680 | tf_op jit(solution)/shard_map/all_to_all | solution.py:31
  25.3 0.1 reshape.35
  25.4 8.6 %fusion.4 = f32[16,2048]{1,0:T(8,128)S(1)} fusion(bf16[16,5120]{1,0:T(8,128)(2,1)S(1)} %reshape.35, bf16[1,5120,2048]{2,1,0:T(8,128)(2,1)} %param.9), kind=kOutput, calls=%fused_computation.5 | convolution fusion | flops 335544320 | bytes 21266432 | tf_op jit(solution)/shard_map/dot_general | solution.py:35
  33.9 4.3 %copy-done = bf16[1,5120,2048]{2,1,0:T(8,128)(2,1)S(1)} copy-done((bf16[1,5120,2048]{2,1,0:T(8,128)(2,1)S(1)}, bf16[1,5120,2048]{2,1,0:T(8,128)(2,1)}, u32[]{:S(2)}) %copy-start) | copy-done | bytes 20971544
  38.3 2.8 %fusion.9 = bf16[16,2048]{1,0:T(8,128)(2,1)S(1)} fusion(bf16[16,5120]{1,0:T(8,128)(2,1)S(1)} %reshape.35, bf16[1,5120,2048]{2,1,0:T(8,128)(2,1)S(1)} %copy-done, f32[16,2048]{1,0:T(8,128)S(1)} %fusion.4), kind=kOutput, calls=%fused_computation.9 | convolution fusion | flops 335740928 | bytes 21331968 | tf_op jit(solution)/shard_map/dot_general | solution.py:36
  41.1 0.1 dot_general.17
  41.2 8.4 %fusion = f32[8,2,5120]{2,0,1:T(8,128)S(1)} fusion(bf16[1,2048,5120]{2,1,0:T(8,128)(2,1)} %param.11, bf16[8,2,2048]{2,1,0:T(2,128)(2,1)S(1)} %dot_general.17), kind=kOutput, calls=%fused_computation.1 | convolution fusion | flops 335544320 | bytes 21364736 | tf_op jit(solution)/shard_map/dot_general | solution.py:38
  49.6 1.0 %copy.13 = f32[8,2,5120]{2,1,0:T(2,128)} copy(f32[8,2,5120]{2,0,1:T(8,128)S(1)} %fusion) | data formatting | bytes 655360 | tf_op jit(solution)/shard_map/dot_general | solution.py:38
  50.6 3.4 %all-to-all-start.1 = ((f32[8,2,5120]{2,1,0:T(2,128)}), f32[8,2,5120]{2,1,0:T(2,128)S(1)}, u32[]{:S(2)}, u32[]{:S(2)}) async-start(f32[8,2,5120]{2,1,0:T(2,128)} %copy.13), calls=%async_computation.1 | async-start | bytes 655360 | tf_op jit(solution)/shard_map/all_to_all | solution.py:40
  54.0 0.0 reduce-scatter.4.cloned.1.call-start
  54.1 9.5 %all-to-all-done.1 = f32[8,2,5120]{2,1,0:T(2,128)S(1)} async-done(((f32[8,2,5120]{2,1,0:T(2,128)}), f32[8,2,5120]{2,1,0:T(2,128)S(1)}, u32[]{:S(2)}, u32[]{:S(2)}) %all-to-all-start.1) | async-done | bytes 327712 | tf_op jit(solution)/shard_map/all_to_all | solution.py:40
  63.6 0.1 bitcast_reduce_fusion
  63.8 0.1 reshape.37
  63.9 0.6 gather_fusion
  64.5 0.1 broadcast_select_fusion
  64.6 2.3 %copy.16 = f32[4,5120]{0,1:T(8,128)} copy(f32[4,5120]{1,0:T(4,128)S(1)} %broadcast_select_fusion) | data formatting | bytes 163840
  66.9 9.4 %reduce-scatter.4.cloned.1.call-done = f32[2560,4]{1,0:T(8,128)} async-done(((f32[5120,4]{1,0:T(8,128)}), f32[2560,4]{1,0:T(8,128)}) %reduce-scatter.4.cloned.1.call-update) | async-done | bytes 40976
  76.3 1.7 %copy.17 = f32[4,2560]{1,0:T(4,128)S(1)} copy(f32[4,2560]{0,1:T(8,128)} %bitcast.33) | data formatting | bytes 81920
  78.0 0.7 multiply_convert_fusion
  (9 shorter events, 0.1 us)
Async XLA Ops:
  25.3 12.9 %copy-start = (bf16[1,5120,2048]{2,1,0:T(8,128)(2,1)S(1)}, bf16[1,5120,2048]{2,1,0:T(8,128)(2,1)}, u32[]{:S(2)}) copy-start(bf16[1,5120,2048]{2,1,0:T(8,128)(2,1)} %param.10) | copy-start | bytes 62914564
  38.3 15.8 %copy-start.2 = (s32[4,1]{0,1:T(1,128)S(1)}, s32[4,1]{0,1:T(1,128)}, u32[]{:S(2)}) copy-start(s32[4,1]{0,1:T(1,128)} %param.7) | copy-start | bytes 52
  41.1 36.9 %copy-start.1 = (f32[4]{0:T(128)S(1)}, f32[4]{0:T(128)}, u32[]{:S(2)}) copy-start(f32[4]{0:T(128)} %param.8) | copy-start | bytes 52
  50.6 13.0 %all-to-all-start.1 = ((f32[8,2,5120]{2,1,0:T(2,128)}), f32[8,2,5120]{2,1,0:T(2,128)S(1)}, u32[]{:S(2)}, u32[]{:S(2)}) async-start(f32[8,2,5120]{2,1,0:T(2,128)} %copy.13), calls=%async_computation.1 | async-start | bytes 655360 | tf_op jit(solution)/shard_map/all_to_all | solution.py:40
  54.0 22.3 %reduce-scatter.4.cloned.1.call-start = ((), (), s32[]{:S(2)}) async-start(), calls=%async_computation.3 | async-start | bytes 3932160
Sparse Core Ops, SparseCore 0:
  67.0 9.2 reduce-scatter.3
where the time goes:
time: 85.9 us; the launch traced here: 85.6 us
  matrix products  20 us (23%)
  waiting for transfers between devices  19 us (22%)
  blocking collectives  16.9 us (20%)
  between operations  13.5 us (16%)
  local copies, waits for them, and re-layouts  10.3 us (12%)
  starting transfers between devices  3.47 us (4%)
  other arithmetic  2.49 us (3%)
    all_to_all x1, blocking collectives, local(): lax.all_to_all(jnp.repeat(placed, per_expert, axis=0), 'expert', split_ax...  14.7 us
    all_to_all x1, waiting for transfers between devices, local(): lax.all_to_all(partial_value, 'expert', split_axis=0, concat_axis=0, tile...  9.52 us
    unnamed x2, waiting for transfers between devices  9.45 us
    dot_general x1, matrix products, local(): gate = jnp.dot(flat, w_gate, preferred_element_type=jnp.float32)  8.58 us
    dot_general x1, matrix products, local(): partial_value = jnp.dot(hidden, w_down, preferred_element_type=jnp.float32)  8.42 us
    unnamed x8, local copies, waits for them, and re-layouts  8.37 us
    all_to_all x1, starting transfers between devices, local(): lax.all_to_all(partial_value, 'expert', split_axis=0, concat_axis=0, tile...  3.43 us
    dot_general x1, matrix products, local(): up_part = jnp.dot(flat, w_up, preferred_element_type=jnp.float32)  2.82 us
  transfers between devices with their start and end apart: 2, of which 2 were waited for; matrix products, arithmetic and copies ran while one was open for 0% of the time, Pallas kernels for 0%

commit v1 on v0

v1 whole, which is shorter than its diff:
```python
import functools

import jax
import jax.numpy as jnp
from jax import lax
from jax.experimental import pallas as pl
from jax.experimental.pallas import tpu as pltpu
from jax.sharding import PartitionSpec as P

NE = 4
CAP = 2
MESH = pl.DeviceIdType.MESH
F32 = jnp.float32
BF16 = jnp.bfloat16


def chunk_of(size):
    for width in (512, 256, 128):
        if size % width == 0:
            return width
    return size


def groups_of(count):
    first = (count + 1) // 2
    return [g for g in (first, count - first) if g]


def each(count, body):
    for i in range(count):
        body(i)


def kernel(
    n, ids_ref, scale_ref, tok_ref, gate_ref, up_ref, down_ref, out_ref,
    w_gate, w_up, w_down, placed, snd, recv, rows32, flat_own, flat_other,
    acc_gate, acc_up, hidden, cross_out, cross_in, part32, summed, osnd0, orecv0, osnd1, orecv1,
    gate_sem, up_sem, down_sem, snd_sem, recv_sem, flat_sem, cross_ssem, cross_rsem, out_ssem, out_rsem,
):
    me = lax.axis_index("expert")
    core = lax.axis_index("tensor")
    other = 1 - core
    per = n // NE
    tok_rows, half = tok_ref.shape
    chunk = flat_own.shape[2]
    nc = half // chunk
    groups = groups_of(nc)
    osnd, orecv = (osnd0, osnd1), (orecv0, orecv1)

    def peer(d):
        return lax.rem(me + d, n)

    barrier = pltpu.get_barrier_semaphore()
    pl.semaphore_signal(barrier, inc=1, device_id={"tensor": other}, device_id_type=MESH)

    @pl.loop(1, n)
    def _(d):
        pl.semaphore_signal(barrier, inc=1, device_id={"expert": peer(d)}, device_id_type=MESH)

    def row_of(c):
        side = jnp.where(c < nc, core, other)
        return pl.multiple_of((side * nc + lax.rem(c, nc)) * chunk, chunk)

    def col_of(c):
        side = jnp.where(c < nc, other, core)
        return pl.multiple_of((side * nc + lax.rem(c, nc)) * chunk, chunk)

    def gate_copy(c):
        return pltpu.make_async_copy(gate_ref.at[0, pl.ds(row_of(c), chunk), :], w_gate.at[c], gate_sem.at[c])

    def up_copy(c):
        return pltpu.make_async_copy(up_ref.at[0, pl.ds(row_of(c), chunk), :], w_up.at[c], up_sem.at[c])

    def down_copy(c):
        return pltpu.make_async_copy(down_ref.at[0, :, pl.ds(col_of(c), chunk)], w_down.at[c], down_sem.at[c])

    @pl.loop(0, 2 * nc)
    def _(c):
        gate_copy(c).start()
        up_copy(c).start()

    ids = [ids_ref[i, 0] for i in range(tok_rows)]
    keys = []
    for i in range(tok_rows):
        slot = jnp.int32(0)
        for j in range(i):
            slot = slot + (ids[j] == ids[i]).astype(jnp.int32)
        keys.append(ids[i] * CAP + slot)
    tok = tok_ref[...].astype(F32)
    slots = lax.broadcasted_iota(jnp.int32, (NE * CAP, 1), 0)
    total = jnp.zeros((NE * CAP, half), F32)
    for i in range(tok_rows):
        total = total + jnp.where(slots == keys[i], 1.0, 0.0).astype(F32) * tok[i : i + 1, :]
    placed[...] = total
    for e in range(NE):
        snd[e] = placed[e * CAP : (e + 1) * CAP, :].astype(BF16)

    pl.semaphore_wait(barrier, n)

    def send_copy(d):
        to = peer(d)
        return pltpu.make_async_remote_copy(
            src_ref=snd.at[to // per], dst_ref=recv.at[me], send_sem=snd_sem.at[d], recv_sem=recv_sem.at[me],
            device_id={"expert": to}, device_id_type=MESH,
        )

    def recv_copy(d):
        source = peer(d)
        return pltpu.make_async_remote_copy(
            src_ref=snd.at[0], dst_ref=recv.at[source], send_sem=snd_sem.at[d], recv_sem=recv_sem.at[source],
            device_id={"expert": source}, device_id_type=MESH,
        )

    @pl.loop(1, n)
    def _(d):
        send_copy(d).start()

    @pl.loop(0, 2 * nc)
    def _(c):
        down_copy(c).start()

    recv[me] = snd[me // per]

    @pl.loop(1, n)
    def _(d):
        recv_copy(d).wait_recv()

    def unpack(i):
        rows32[pl.ds(i * CAP, CAP), :] = recv[i].astype(F32)

    each(n, unpack)
    for c in range(nc):
        flat_own[c] = rows32[:, c * chunk : (c + 1) * chunk].astype(BF16)
    flat_copy = pltpu.make_async_remote_copy(
        src_ref=flat_own, dst_ref=flat_other, send_sem=flat_sem.at[0], recv_sem=flat_sem.at[1],
        device_id={"tensor": other}, device_id_type=MESH,
    )
    flat_copy.start()

    acc_gate[...] = jnp.zeros_like(acc_gate)
    acc_up[...] = jnp.zeros_like(acc_up)

    def gate_up(flat, base):
        @pl.loop(0, nc)
        def _(c):
            lhs = flat[c]
            gate_copy(base + c).wait()
            acc_gate[...] += jnp.dot(lhs, w_gate[base + c], preferred_element_type=F32)
            up_copy(base + c).wait()
            acc_up[...] += jnp.dot(lhs, w_up[base + c], preferred_element_type=F32)

    gate_up(flat_own, 0)
    flat_copy.wait_recv()
    gate_up(flat_other, nc)
    value = acc_gate[...]
    hidden[...] = (value / (1.0 + jnp.exp(-value)) * acc_up[...]).astype(BF16)

    def cross_copy(c):
        return pltpu.make_async_remote_copy(
            src_ref=cross_out.at[c], dst_ref=cross_in.at[c], send_sem=cross_ssem.at[c], recv_sem=cross_rsem.at[c],
            device_id={"tensor": other}, device_id_type=MESH,
        )

    @pl.loop(0, nc)
    def _(c):
        down_copy(c).wait()
        cross_out[c] = jnp.dot(hidden[...], w_down[c], preferred_element_type=F32)
        cross_copy(c).start()

    def out_copy(g, d, source):
        to = peer(d)
        row = to if source else me
        return pltpu.make_async_remote_copy(
            src_ref=osnd[g].at[to], dst_ref=orecv[g].at[row],
            send_sem=out_ssem.at[g, d], recv_sem=out_rsem.at[g, row],
            device_id={"expert": to}, device_id_type=MESH,
        )

    first = 0
    for g, count in enumerate(groups):
        for c in range(count):
            at = nc + first + c
            down_copy(at).wait()
            result = jnp.dot(hidden[...], w_down[at], preferred_element_type=F32)
            cross_copy(first + c).wait_recv()
            part32[:, c * chunk : (c + 1) * chunk] = result + cross_in[first + c]

        def pack(i, g=g, count=count):
            osnd[g][i] = part32[pl.ds(i * CAP, CAP), : count * chunk].astype(BF16)

        each(n, pack)

        @pl.loop(1, n)
        def _(d, g=g):
            out_copy(g, d, False).start()

        orecv[g][me] = osnd[g][me]
        first += count

    lanes = lax.broadcasted_iota(jnp.int32, (tok_rows, 1), 0)
    key = jnp.zeros((tok_rows, 1), jnp.int32)
    scale = jnp.zeros((tok_rows, 1), F32)
    for i in range(tok_rows):
        key = jnp.where(lanes == i, keys[i], key)
        scale = jnp.where(lanes == i, scale_ref[i], scale)
    first = 0
    for g, count in enumerate(groups):

        @pl.loop(1, n)
        def _(d, g=g):
            out_copy(g, d, True).wait_recv()

        width = count * chunk
        for e in range(NE):
            if per <= 8:
                rows = orecv[g][e * per].astype(F32)
                for j in range(1, per):
                    rows = rows + orecv[g][e * per + j].astype(F32)
                summed[e * CAP : (e + 1) * CAP, :width] = rows
            else:
                summed[e * CAP : (e + 1) * CAP, :width] = jnp.zeros((CAP, width), F32)

                @pl.loop(0, per)
                def _(j, g=g, e=e, width=width):
                    summed[e * CAP : (e + 1) * CAP, :width] += orecv[g][e * per + j].astype(F32)

        mine = jnp.zeros((tok_rows, width), F32)
        for r in range(NE * CAP):
            mine = mine + jnp.where(key == r, 1.0, 0.0).astype(F32) * summed[r : r + 1, :width]
        out_ref[:, first * chunk : first * chunk + width] = (mine * scale).astype(BF16)
        first += count

    flat_copy.wait_send()

    @pl.loop(1, n)
    def _(d):
        send_copy(d).wait_send()

    @pl.loop(0, nc)
    def _(c):
        cross_copy(c).wait_send()

    for g in range(len(groups)):

        @pl.loop(1, n)
        def _(d, g=g):
            out_copy(g, d, False).wait_send()


def local(tokens, expert_ids, route_scale, gate_weight, up_weight, down_weight):
    n = lax.axis_size("expert")
    tok_rows, half = tokens.shape
    width = gate_weight.shape[2]
    rows = n * CAP
    chunk = chunk_of(half)
    nc = half // chunk
    groups = groups_of(nc)
    sizes = [g * chunk for g in groups]
    if len(sizes) == 1:
        sizes = sizes + sizes
    dma = pltpu.SemaphoreType.DMA
    vmem = pl.BlockSpec(memory_space=pltpu.VMEM)
    smem = pl.BlockSpec(memory_space=pltpu.SMEM)
    hbm = pl.BlockSpec(memory_space=pl.ANY)
    return pl.pallas_call(
        functools.partial(kernel, n),
        out_shape=jax.ShapeDtypeStruct((tok_rows, half), BF16),
        in_specs=[smem, smem, vmem, hbm, hbm, hbm],
        out_specs=vmem,
        scratch_shapes=[
            pltpu.VMEM((2 * nc, chunk, width), BF16),
            pltpu.VMEM((2 * nc, chunk, width), BF16),
            pltpu.VMEM((2 * nc, width, chunk), BF16),
            pltpu.VMEM((NE * CAP, half), F32),
            pltpu.VMEM((NE, CAP, half), BF16),
            pltpu.VMEM((n, CAP, half), BF16),
            pltpu.VMEM((rows, half), F32),
            pltpu.VMEM((nc, rows, chunk), BF16),
            pltpu.VMEM((nc, rows, chunk), BF16),
            pltpu.VMEM((rows, width), F32),
            pltpu.VMEM((rows, width), F32),
            pltpu.VMEM((rows, width), BF16),
            pltpu.VMEM((nc, rows, chunk), F32),
            pltpu.VMEM((nc, rows, chunk), F32),
            pltpu.VMEM((rows, sizes[0]), F32),
            pltpu.VMEM((NE * CAP, sizes[0]), F32),
            pltpu.VMEM((n, CAP, sizes[0]), BF16),
            pltpu.VMEM((n, CAP, sizes[0]), BF16),
            pltpu.VMEM((n, CAP, sizes[1]), BF16),
            pltpu.VMEM((n, CAP, sizes[1]), BF16),
            dma((2 * nc,)),
            dma((2 * nc,)),
            dma((2 * nc,)),
            dma((n,)),
            dma((n,)),
            dma((2,)),
            dma((nc,)),
            dma((nc,)),
            dma((2, n)),
            dma((2, n)),
        ],
        compiler_params=pltpu.CompilerParams(
            collective_id=0, has_side_effects=True, vmem_limit_bytes=66_900_000
        ),
        cost_estimate=pl.CostEstimate(
            flops=6 * rows * 2 * half * width, bytes_accessed=12 * half * width, transcendentals=rows * width
        ),
    )(expert_ids, route_scale, tokens, gate_weight, up_weight, down_weight)


def solution(mesh):
    in_specs = (
        P(("group", "expert"), "tensor"),
        P(("group", "expert"), None),
        P(("group", "expert")),
        P("expert", None, "tensor"),
        P("expert", None, "tensor"),
        P("expert", "tensor", None),
    )
    out_specs = P(("group", "expert"), "tensor")
    return jax.shard_map(local, mesh=mesh, in_specs=in_specs, out_specs=out_specs, check_vma=False)
```

time: 85.9 us -> 32.7 us (0.38)
  Pallas kernels: 0 us -> 29.8 us
  matrix products: 20 us -> 0 us
  waiting for transfers between devices: 19 us -> 0 us
  blocking collectives: 16.9 us -> 0 us
  between operations: 13.5 us -> 0.01 us
  local copies, waits for them, and re-layouts: 10.3 us -> 2.65 us
  starting transfers between devices: 3.47 us -> 0 us
  other arithmetic: 2.49 us -> 0 us
    pallas_call x0 -> x1, Pallas kernels: none -> 29.8 us  [local(): pl.pallas_call(functools.partial(kernel, n), out_shape=jax.ShapeDtypeStru...]
    dot_general x4 -> x0, matrix products: 20 us -> none  [the longest x1 8.58 us: local(): gate = jnp.dot(flat, w_gate, preferred_element_type=jnp.float32)]
    all_to_all x1 -> x0, blocking collectives: 14.7 us -> none  [local(): lax.all_to_all(jnp.repeat(placed, per_expert, axis=0), 'expert', split_ax...]
    all_to_all x1 -> x0, waiting for transfers between devices: 9.52 us -> none  [local(): lax.all_to_all(partial_value, 'expert', split_axis=0, concat_axis=0, tile...]
    unnamed x2 -> x0, waiting for transfers between devices: 9.45 us -> none
    unnamed x8 -> x2, local copies, waits for them, and re-layouts: 8.37 us -> 2.65 us
    all_to_all x1 -> x0, starting transfers between devices: 3.43 us -> none  [local(): lax.all_to_all(partial_value, 'expert', split_axis=0, concat_axis=0, tile...]
    all_gather x1 -> x0, blocking collectives: 2.14 us -> none  [local(): whole = lax.all_gather(tokens, 'tensor', axis=1, tiled=True)]
  transfers between devices with their start and end apart: 2 -> 0, of which waited for: 2 -> 0; matrix products, arithmetic and copies ran while one was open for 0% -> 0% of each run, Pallas kernels for 0% -> 0%
where the time goes in v1:
time: 32.7 us; the launch traced here: 32.5 us
  Pallas kernels  29.8 us (91%)
  local copies, waits for them, and re-layouts  2.65 us (8%)
    pallas_call x1, Pallas kernels, local(): pl.pallas_call(functools.partial(kernel, n), out_shape=jax.ShapeDtypeStru...  29.8 us
    unnamed x2, local copies, waits for them, and re-layouts  2.65 us

profile of v1, /device:TPU:0, one launch (start us, length us, event | category | flops | bytes accessed | tf_op | source)
XLA Modules:
  0.0 32.5 jit_solution(4759953453006851233)
XLA Ops:
  0.0 1.3 %copy.7.ids_ref = s32[4,1]{1,0:T(4,128)} copy(s32[4,1]{0,1:T(1,128)} %param.7) | data formatting | bytes 32 | tf_op args[1]
  1.3 29.8 %shard_map.64 = bf16[4,2560]{1,0:T(4,128)(2,1)} custom-call(s32[4,1]{1,0:T(4,128)} %copy.7.ids_ref, f32[4]{0:T(128)} %scale_ref.1, bf16[4,2560]{1,0:T(4,128)(2,1)} %tok_ref.1, bf16[1,5120,2048]{2,1,0:T(8,128)(2,1)} %gate_ref.1, bf16[1,5120,2048]{2,1,0:T(8,128)(2,1)} %up_ref.1, bf16[1,2048,5120]{2,1,0:T(8,128)(2,1)} %down_ref.1), custom_call_target="tpu_custom_call" | custom-call | flops 1006632960 | bytes 62914560 | tf_op jit(solution)/shard_map/pallas_call | solution.py:265
  31.1 1.3 %copy.9 = bf16[4,2560]{1,0:T(4,128)(2,1)} copy(bf16[4,2560]{1,0:T(4,128)(2,1)} %shard_map.64) | data formatting | bytes 40960

commit v2 on v1

--- a/solution.py
+++ b/solution.py
@@ -32,7 +32,7 @@
 
 
 def kernel(
-    n, ids_ref, scale_ref, tok_ref, gate_ref, up_ref, down_ref, out_ref,
+    n, ids_ref, tok_ref, gate_ref, up_ref, down_ref, out_ref,
     w_gate, w_up, w_down, placed, snd, recv, rows32, flat_own, flat_other,
     acc_gate, acc_up, hidden, cross_out, cross_in, part32, summed, osnd0, orecv0, osnd1, orecv1,
     gate_sem, up_sem, down_sem, snd_sem, recv_sem, flat_sem, cross_ssem, cross_rsem, out_ssem, out_rsem,
@@ -79,7 +79,7 @@
         gate_copy(c).start()
         up_copy(c).start()
 
-    ids = [ids_ref[i, 0] for i in range(tok_rows)]
+    ids = [ids_ref[i] for i in range(tok_rows)]
     keys = []
     for i in range(tok_rows):
         slot = jnp.int32(0)
@@ -199,10 +199,8 @@
 
     lanes = lax.broadcasted_iota(jnp.int32, (tok_rows, 1), 0)
     key = jnp.zeros((tok_rows, 1), jnp.int32)
-    scale = jnp.zeros((tok_rows, 1), F32)
     for i in range(tok_rows):
         key = jnp.where(lanes == i, keys[i], key)
-        scale = jnp.where(lanes == i, scale_ref[i], scale)
     first = 0
     for g, count in enumerate(groups):
 
@@ -227,7 +225,7 @@
         mine = jnp.zeros((tok_rows, width), F32)
         for r in range(NE * CAP):
             mine = mine + jnp.where(key == r, 1.0, 0.0).astype(F32) * summed[r : r + 1, :width]
-        out_ref[:, first * chunk : first * chunk + width] = (mine * scale).astype(BF16)
+        out_ref[:, first * chunk : first * chunk + width] = mine
         first += count
 
     flat_copy.wait_send()
@@ -262,10 +260,10 @@
     vmem = pl.BlockSpec(memory_space=pltpu.VMEM)
     smem = pl.BlockSpec(memory_space=pltpu.SMEM)
     hbm = pl.BlockSpec(memory_space=pl.ANY)
-    return pl.pallas_call(
+    summed = pl.pallas_call(
         functools.partial(kernel, n),
-        out_shape=jax.ShapeDtypeStruct((tok_rows, half), BF16),
-        in_specs=[smem, smem, vmem, hbm, hbm, hbm],
+        out_shape=jax.ShapeDtypeStruct((tok_rows, half), F32),
+        in_specs=[smem, vmem, hbm, hbm, hbm],
         out_specs=vmem,
         scratch_shapes=[
             pltpu.VMEM((2 * nc, chunk, width), BF16),
@@ -305,7 +303,8 @@
         cost_estimate=pl.CostEstimate(
             flops=6 * rows * 2 * half * width, bytes_accessed=12 * half * width, transcendentals=rows * width
         ),
-    )(expert_ids, route_scale, tokens, gate_weight, up_weight, down_weight)
+    )(expert_ids.reshape(tok_rows), tokens, gate_weight, up_weight, down_weight)
+    return (summed * route_scale[:, None]).astype(BF16)
 
 
 def solution(mesh):

time: 32.7 us -> 31.6 us (0.966)
  local copies, waits for them, and re-layouts: 2.65 us -> 0.01 us
  other arithmetic: 0 us -> 1.46 us
    unnamed x2, local copies, waits for them, and re-layouts: 2.65 us -> 0.01 us
    convert_element_type x0 -> x1, other arithmetic: none -> 1.46 us  [local(): return (summed * route_scale[:, None]).astype(BF16)]
where the time goes in v2:
time: 31.6 us; the launch traced here: 31.4 us
  Pallas kernels  29.9 us (95%)
  other arithmetic  1.46 us (5%)
    pallas_call x1, Pallas kernels, local(): pl.pallas_call(functools.partial(kernel, n), out_shape=jax.ShapeDtypeStru...  29.9 us
    convert_element_type x1, other arithmetic, local(): return (summed * route_scale[:, None]).astype(BF16)  1.46 us

profile of v2, /device:TPU:0, one launch (start us, length us, event | category | flops | bytes accessed | tf_op | source)
XLA Modules:
  0.0 31.4 jit_solution(11235427459152164614)
XLA Ops:
  0.0 0.0 copy-start
  0.0 29.9 %shard_map.64 = f32[4,2560]{1,0:T(4,128)} custom-call(s32[4]{0:T(128)} %bitcast.1, bf16[4,2560]{1,0:T(4,128)(2,1)} %tok_ref.1, bf16[1,5120,2048]{2,1,0:T(8,128)(2,1)} %gate_ref.1, bf16[1,5120,2048]{2,1,0:T(8,128)(2,1)} %up_ref.1, bf16[1,2048,5120]{2,1,0:T(8,128)(2,1)} %down_ref.1), custom_call_target="tpu_custom_call" | custom-call | flops 1006632960 | bytes 62914560 | tf_op jit(solution)/shard_map/pallas_call | solution.py:263
  29.9 0.0 copy-done
  29.9 1.5 %multiply_convert_fusion = bf16[4,2560]{1,0:T(4,128)(2,1)} fusion(f32[4,2560]{1,0:T(4,128)} %shard_map.64, f32[4]{0:T(128)S(1)} %copy-done), kind=kLoop, calls=%fused_computation | loop fusion | flops 20480 | bytes 61456 | tf_op jit(solution)/shard_map/convert_element_type | solution.py:307
Async XLA Ops:
  0.0 29.9 %copy-start = (f32[4]{0:T(128)S(1)}, f32[4]{0:T(128)}, u32[]{:S(2)}) copy-start(f32[4]{0:T(128)} %param.8) | copy-start | bytes 52

commit v3 on v2

--- a/solution.py
+++ b/solution.py
@@ -22,7 +22,7 @@
 
 
 def groups_of(count):
-    first = (count + 1) // 2
+    first = max(count - 1, 1)
     return [g for g in (first, count - first) if g]
 
 
@@ -50,6 +50,27 @@
     def peer(d):
         return lax.rem(me + d, n)
 
+    def row_of(c):
+        side = jnp.where(c < nc, core, other)
+        return pl.multiple_of((side * nc + lax.rem(c, nc)) * chunk, chunk)
+
+    def col_of(c):
+        side = jnp.where(c < nc, other, core)
+        return pl.multiple_of((side * nc + lax.rem(c, nc)) * chunk, chunk)
+
+    def gate_copy(c):
+        return pltpu.make_async_copy(gate_ref.at[0, pl.ds(row_of(c), chunk), :], w_gate.at[c], gate_sem.at[c])
+
+    def up_copy(c):
+        return pltpu.make_async_copy(up_ref.at[0, pl.ds(row_of(c), chunk), :], w_up.at[c], up_sem.at[c])
+
+    def down_copy(c):
+        return pltpu.make_async_copy(down_ref.at[0, :, pl.ds(col_of(c), chunk)], w_down.at[c], down_sem.at[c])
+
+    for c in range(2):
+        gate_copy(c).start()
+        up_copy(c).start()
+
     barrier = pltpu.get_barrier_semaphore()
     pl.semaphore_signal(barrier, inc=1, device_id={"tensor": other}, device_id_type=MESH)
 
@@ -57,24 +78,7 @@
     def _(d):
         pl.semaphore_signal(barrier, inc=1, device_id={"expert": peer(d)}, device_id_type=MESH)
 
-    def row_of(c):
-        side = jnp.where(c < nc, core, other)
-        return pl.multiple_of((side * nc + lax.rem(c, nc)) * chunk, chunk)
-
-    def col_of(c):
-        side = jnp.where(c < nc, other, core)
-        return pl.multiple_of((side * nc + lax.rem(c, nc)) * chunk, chunk)
-
-    def gate_copy(c):
-        return pltpu.make_async_copy(gate_ref.at[0, pl.ds(row_of(c), chunk), :], w_gate.at[c], gate_sem.at[c])
-
-    def up_copy(c):
-        return pltpu.make_async_copy(up_ref.at[0, pl.ds(row_of(c), chunk), :], w_up.at[c], up_sem.at[c])
-
-    def down_copy(c):
-        return pltpu.make_async_copy(down_ref.at[0, :, pl.ds(col_of(c), chunk)], w_down.at[c], down_sem.at[c])
-
-    @pl.loop(0, 2 * nc)
+    @pl.loop(2, 2 * nc)
     def _(c):
         gate_copy(c).start()
         up_copy(c).start()

time: 31.6 us -> 31.5 us (level)
  no operation moved by 1% of the time
where the time goes in v3:
time: 31.5 us; the launch traced here: 31.3 us
  Pallas kernels  29.8 us (95%)
  other arithmetic  1.46 us (5%)
    pallas_call x1, Pallas kernels, local(): pl.pallas_call(functools.partial(kernel, n), out_shape=jax.ShapeDtypeStru...  29.8 us
    convert_element_type x1, other arithmetic, local(): return (summed * route_scale[:, None]).astype(BF16)  1.46 us

profile of v3, /device:TPU:0, one launch (start us, length us, event | category | flops | bytes accessed | tf_op | source)
XLA Modules:
  0.0 31.3 jit_solution(5813790313606123748)
XLA Ops:
  0.0 0.0 copy-start
  0.0 29.8 %shard_map.64 = f32[4,2560]{1,0:T(4,128)} custom-call(s32[4]{0:T(128)} %bitcast.1, bf16[4,2560]{1,0:T(4,128)(2,1)} %tok_ref.1, bf16[1,5120,2048]{2,1,0:T(8,128)(2,1)} %gate_ref.1, bf16[1,5120,2048]{2,1,0:T(8,128)(2,1)} %up_ref.1, bf16[1,2048,5120]{2,1,0:T(8,128)(2,1)} %down_ref.1), custom_call_target="tpu_custom_call" | custom-call | flops 1006632960 | bytes 62914560 | tf_op jit(solution)/shard_map/pallas_call | solution.py:267
  29.8 0.0 copy-done
  29.8 1.5 %multiply_convert_fusion = bf16[4,2560]{1,0:T(4,128)(2,1)} fusion(f32[4,2560]{1,0:T(4,128)} %shard_map.64, f32[4]{0:T(128)S(1)} %copy-done), kind=kLoop, calls=%fused_computation | loop fusion | flops 20480 | bytes 61456 | tf_op jit(solution)/shard_map/convert_element_type | solution.py:311
Async XLA Ops:
  0.0 29.8 %copy-start = (f32[4]{0:T(128)S(1)}, f32[4]{0:T(128)}, u32[]{:S(2)}) copy-start(f32[4]{0:T(128)} %param.8) | copy-start | bytes 52
